TPU v7x, 32 devices: a whole 2x2x4 slice. The times are simulated.
32 devices in a mesh: blk: 8 (over z, y), rep: 4 (over x, core).
Axes of the slice: x: 2, y: 2, z: 4, core: 2. Of those that a mesh axis runs over, the one named last changes fastest.
Arguments:
- tensor_blocks: bfloat16 [64, 128, 128, 128], P(('blk', 'rep')), may hold values from -15 to 15
- triples: int32 [64, 3], P(('blk', 'rep')), may hold values from 0 to 15, as said below
- slot_count: int32 [32], P(('blk', 'rep')), may hold values from 1 to 2, as said below
- factor: bfloat16 [2048, 256], P('blk', 'rep'), may hold values from -0.34375 to 0.34375
Outputs:
- gradient: float32 [2048, 256], P('blk', 'rep')
Inputs may be any that keep to these rules, and one draw needn't show every extreme that they name: `triples`: each row is i >= j >= k; equal indices occur; the different row blocks named by the 2 slots of one device have different values of block // 2. `slot_count`: the first device's entry is 2.
All inputs are finite; a program needn't handle non-finite values.
Results may differ from a plain program's by a relative error of at most 0.003.
Values may be sent and summed in bfloat16 or wider, within the bound.
A program may use at most 128 MiB of HBM per device.

v0:
```python
import jax
import jax.numpy as jnp
from jax import lax
from jax.sharding import PartitionSpec as P


def side_weights(triples):
    first_idx = triples[:, 0]
    second_idx = triples[:, 1]
    third_idx = triples[:, 2]
    same_upper = first_idx == second_idx
    same_lower = second_idx == third_idx
    apart = jnp.logical_and(jnp.logical_not(same_upper), jnp.logical_not(same_lower))
    every = jnp.logical_and(same_upper, same_lower)
    base = jnp.where(apart, 2.0, 1.0).astype(jnp.float32)
    dropped = jnp.where(every, 0.0, base)
    return jnp.stack([base, dropped, dropped], axis=1)


def contract(block, upper, middle, lower):
    edge_size = block.shape[0]
    rank_width = upper.shape[1]
    by_lower = jnp.dot(
        block.reshape(edge_size * edge_size, edge_size), lower, preferred_element_type=jnp.float32
    ).reshape(edge_size, edge_size, rank_width)
    by_upper = lax.dot_general(
        block.reshape(edge_size, edge_size * edge_size),
        upper,
        (((0,), (0,)), ((), ())),
        preferred_element_type=jnp.float32,
    ).reshape(edge_size, edge_size, rank_width)
    upper_wide = upper.astype(jnp.float32)
    middle_wide = middle.astype(jnp.float32)
    to_first = jnp.einsum("abr,br->ar", by_lower, middle_wide, precision=lax.Precision.HIGHEST)
    to_second = jnp.einsum("abr,ar->br", by_lower, upper_wide, precision=lax.Precision.HIGHEST)
    to_third = jnp.einsum("bcr,br->cr", by_upper, middle_wide, precision=lax.Precision.HIGHEST)
    return (to_first, to_second, to_third)


def owned_table(listed, owner_count, per_owner):
    myself = lax.axis_index("blk")
    flat = listed.reshape(owner_count, -1)
    mine = flat // per_owner == myself
    local = flat % per_owner
    column_ids = jnp.arange(per_owner, dtype=jnp.int32)
    hits = jnp.logical_and(mine[:, :, None], local[:, :, None] == column_ids[None, None, :])
    return jnp.any(hits, axis=1)


def shards(tensor_blocks, triples, slot_count, factor):
    own_rows = lax.all_gather(factor, "rep", axis=1, tiled=True)
    block_size = tensor_blocks.shape[1]
    rank_width = own_rows.shape[1]
    owner_count = lax.axis_size("blk")
    per_owner = own_rows.shape[0] // block_size
    block_count = owner_count * per_owner
    gathered = lax.all_gather(own_rows, "blk", axis=0, tiled=True)
    table = gathered.reshape(block_count, block_size, rank_width)
    divisor = 1
    gram_matrix = lax.dot_general(
        gathered, gathered, (((0,), (0,)), ((), ())), preferred_element_type=jnp.float32
    )
    slot_total = tensor_blocks.shape[0]
    alive = (jnp.arange(slot_total, dtype=jnp.int32) < slot_count[0]).astype(jnp.float32)
    weights = side_weights(triples) * alive[:, None]
    results = []
    for slot_index in range(slot_total):
        triple = triples[slot_index]
        upper = table[triple[0] // divisor]
        middle = table[triple[1] // divisor]
        lower = table[triple[2] // divisor]
        results.extend(contract(tensor_blocks[slot_index], upper, middle, lower))
    stacked = jnp.stack(results, axis=0)
    targets = triples.reshape(-1)
    flat_weights = weights.reshape(-1)
    hadamard = gram_matrix * gram_matrix
    column_width = factor.shape[1]
    column_start = lax.axis_index("rep") * column_width
    hadamard_cols = lax.dynamic_slice_in_dim(hadamard, column_start, column_width, 1)
    fitted = jnp.dot(
        own_rows.astype(jnp.float32),
        hadamard_cols,
        preferred_element_type=jnp.float32,
        precision=lax.Precision.HIGHEST,
    )
    owner_ids = jnp.arange(owner_count, dtype=jnp.int32)
    routing = (owner_ids[:, None] == (targets // per_owner)[None, :]).astype(jnp.float32)
    routing = routing * flat_weights[None, :]
    outgoing_sums = jnp.einsum("pm,mar->par", routing, stacked, precision=lax.Precision.HIGHEST)
    arrived = lax.all_to_all(outgoing_sums, "blk", split_axis=0, concat_axis=0, tiled=True)
    listed_back = lax.all_gather(triples, "blk", axis=0, tiled=True)
    placing = owned_table(listed_back, owner_count, per_owner).astype(jnp.float32)
    owned = jnp.einsum("ql,qar->lar", placing, arrived, precision=lax.Precision.HIGHEST).reshape(
        per_owner * block_size, rank_width
    )
    owned_sum = lax.psum_scatter(owned, "rep", scatter_dimension=1, tiled=True)
    return fitted - owned_sum


def solution(mesh):
    in_specs = (
        P(("blk", "rep"), None, None, None),
        P(("blk", "rep"), None),
        P(("blk", "rep")),
        P("blk", "rep"),
    )
    out_specs = P("blk", "rep")
    return jax.shard_map(shards, mesh=mesh, in_specs=in_specs, out_specs=out_specs, check_vma=False)
```

profile of v0, /device:TPU:0, one launch (start us, length us, event | category | flops | bytes accessed | tf_op | source)
XLA Modules:
  0.0 226.4 jit_solution(4553768582413507420)
XLA Ops:
  6.5 8.3 %all_gather.9 = bf16[256,256]{0,1:T(8,128)(2,1)} all-gather(bf16[256,64]{0,1:T(8,128)(2,1)} %param.7), channel_id=1, replica_groups=mesh['blk'=8,'rep'=4] {'rep'}, dimensions={1}, use_global_device_ids=true | all-gather | bytes 163840 | tf_op jit(solution)/shard_map/all_gather | solution.py:51
  14.9 0.8 reshape.132
  15.6 1.6 fusion.33
  25.4 0.9 and_select_fusion.1
  30.3 6.0 %fusion.32 = (bf16[1,128,128,128]{3,2,1,0:T(8,128)(2,1)}, bf16[1,128,128,128]{3,2,1,0:T(8,128)(2,1)}) fusion(bf16[2,128,128,128]{3,2,1,0:T(8,128)(2,1)} %param.4), kind=kLoop, calls=%fused_computation.67 | loop fusion | bytes 16777216 | tf_op jit(solution)/shard_map/slice | solution.py:72
  36.3 18.7 %all-gather.3.cloned.1.call-done = bf16[2048,256]{0,1:T(8,128)(2,1)} async-done(((bf16[256,256]{0,1:T(8,128)(2,1)}), bf16[2048,256]{0,1:T(8,128)(2,1)}) %all-gather.3.cloned.1.call-update) | async-done | bytes 1048592 | tf_op jit(solution)/shard_map/all_gather | solution.py:57
  55.0 1.5 copy.24
  57.0 4.6 %convolution_bitcast_fusion.3 = f32[32,8,128,128]{3,1,2,0:T(8,128)S(1)} fusion(bf16[16384,128]{1,0:T(8,128)(2,1)} %bitcast.125, bf16[16,128,256]{2,1,0:T(8,128)(2,1)S(1)} %bitcast.128, s32[]{:T(128)S(6)} %select_n.75), kind=kOutput, calls=%fused_computation.9 | convolution fusion | flops 1073741824 | bytes 21037060 | tf_op jit(solution)/shard_map/dot_general | solution.py:23
  61.5 3.8 %copy.74 = f32[32,8,128,128]{3,2,1,0:T(8,128)S(1)} copy(f32[32,8,128,128]{3,1,2,0:T(8,128)S(1)} %convolution_bitcast_fusion.3) | data formatting | bytes 33554432
  65.4 5.7 %copy-done = f32[32,8,128,128]{3,2,1,0:T(8,128)} copy-done((f32[32,8,128,128]{3,2,1,0:T(8,128)}, f32[32,8,128,128]{3,2,1,0:T(8,128)S(1)}, u32[]{:S(2)}) %copy-start) | copy-done | bytes 16777240
  71.1 6.1 %multiply_reduce_fusion.4 = f32[256,128]{1,0:T(8,128)S(1)} fusion(f32[256,128]{1,0:T(8,128)S(1)} %copy.69, f32[32,8,128,128]{3,2,1,0:T(8,128)S(1)} %copy.74), kind=kLoop, calls=%fused_computation.4 | loop fusion | flops 8355840 | bytes 17039360
  77.4 8.2 %multiply_reduce_fusion.5 = f32[256,128]{1,0:T(8,128)S(1)} fusion(f32[128,128,256]{1,0,2:T(8,128)} %bitcast.121, f32[256,128]{1,0:T(8,128)S(1)} %copy.68), kind=kLoop, calls=%fused_computation.5 | loop fusion | flops 8355840 | bytes 17039360
  85.8 5.8 %convolution_bitcast_fusion.2 = f32[32,8,128,128]{3,1,2,0:T(8,128)S(1)} fusion(bf16[16,8,128,128]{3,2,1,0:T(8,128)(2,1)} %bitcast.126, bf16[16,128,256]{2,1,0:T(8,128)(2,1)S(1)} %bitcast.129, s32[]{:T(128)S(6)} %select_n.76), kind=kOutput, calls=%fused_computation.8 | convolution fusion | flops 1073741824 | bytes 21037060 | tf_op jit(solution)/shard_map/dot_general | solution.py:26
  91.6 6.7 %copy.76 = f32[32,8,128,128]{3,2,1,0:T(8,128)} copy(f32[32,8,128,128]{3,1,2,0:T(8,128)S(1)} %convolution_bitcast_fusion.2) | data formatting | bytes 33554432
  98.3 7.6 %multiply_reduce_fusion.3 = f32[256,128]{1,0:T(8,128)S(1)} fusion(f32[256,128]{1,0:T(8,128)S(1)} %copy.68, f32[32,8,128,128]{3,2,1,0:T(8,128)} %copy.76), kind=kLoop, calls=%fused_computation.3 | loop fusion | flops 8355840 | bytes 17039360
  106.1 4.6 %convolution_bitcast_fusion.1 = f32[32,8,128,128]{3,1,2,0:T(8,128)S(1)} fusion(bf16[16384,128]{1,0:T(8,128)(2,1)} %bitcast.123, bf16[16,128,256]{2,1,0:T(8,128)(2,1)S(1)} %bitcast.130, s32[]{:T(128)S(6)} %select_n.78), kind=kOutput, calls=%fused_computation.7 | convolution fusion | flops 1073741824 | bytes 21037060 | tf_op jit(solution)/shard_map/dot_general | solution.py:23
  110.7 3.8 %copy.77 = f32[32,8,128,128]{3,2,1,0:T(8,128)S(1)} copy(f32[32,8,128,128]{3,1,2,0:T(8,128)S(1)} %convolution_bitcast_fusion.1) | data formatting | bytes 33554432
  114.5 5.7 %copy-done.1 = f32[32,8,128,128]{3,2,1,0:T(8,128)} copy-done((f32[32,8,128,128]{3,2,1,0:T(8,128)}, f32[32,8,128,128]{3,2,1,0:T(8,128)S(1)}, u32[]{:S(2)}) %copy-start.1) | copy-done | bytes 16777240
  120.2 6.3 %multiply_reduce_fusion.1 = f32[256,128]{1,0:T(8,128)S(1)} fusion(f32[256,128]{1,0:T(8,128)S(1)} %copy.72, f32[32,8,128,128]{3,2,1,0:T(8,128)S(1)} %copy.77), kind=kLoop, calls=%fused_computation.1 | loop fusion | flops 8355840 | bytes 17039360
  126.7 8.2 %multiply_reduce_fusion.2 = f32[256,128]{1,0:T(8,128)S(1)} fusion(f32[128,128,256]{1,0,2:T(8,128)} %bitcast.122, f32[256,128]{1,0:T(8,128)S(1)} %copy.71), kind=kLoop, calls=%fused_computation.2 | loop fusion | flops 8355840 | bytes 17039360
  135.1 5.8 %convolution_bitcast_fusion = f32[32,8,128,128]{3,1,2,0:T(8,128)S(1)} fusion(bf16[16,8,128,128]{3,2,1,0:T(8,128)(2,1)} %bitcast.124, bf16[16,128,256]{2,1,0:T(8,128)(2,1)S(1)} %bitcast.131, s32[]{:T(128)S(6)} %select_n.79), kind=kOutput, calls=%fused_computation.6 | convolution fusion | flops 1073741824 | bytes 21037060 | tf_op jit(solution)/shard_map/dot_general | solution.py:26
  140.9 6.7 %copy.79 = f32[32,8,128,128]{3,2,1,0:T(8,128)} copy(f32[32,8,128,128]{3,1,2,0:T(8,128)S(1)} %convolution_bitcast_fusion) | data formatting | bytes 33554432
  147.6 7.7 %multiply_reduce_fusion = f32[256,128]{1,0:T(8,128)S(1)} fusion(f32[256,128]{1,0:T(8,128)S(1)} %copy.71, f32[32,8,128,128]{3,2,1,0:T(8,128)} %copy.79), kind=kLoop, calls=%fused_computation | loop fusion | flops 8355840 | bytes 17039360
  155.5 1.2 stack.34
  156.7 1.0 fusion.16
  157.7 1.3 copy.25
  159.0 3.6 %all-to-all-start = ((f32[8,128,256]{2,1,0:T(8,128)}), f32[8,128,256]{2,1,0:T(8,128)S(1)}, u32[]{:S(2)}, u32[]{:S(2)}) async-start(f32[8,128,256]{2,1,0:T(8,128)} %copy.25), calls=%async_computation | async-start | bytes 2097152 | tf_op jit(solution)/shard_map/all_to_all | solution.py:90
  162.7 31.0 %all-gather = s32[8,2,3]{2,1,0:T(2,128)S(1)} all-gather(s32[1,2,3]{2,1,0:T(2,128)S(1)} %bitcast.140), channel_id=1, replica_groups=mesh['blk'=8,'rep'=4] {'blk'}, dimensions={0}, use_global_device_ids=true | all-gather | bytes 216 | tf_op jit(solution)/shard_map/all_gather | solution.py:91
  194.7 0.6 fusion.24
  195.3 0.7 copy.90
  196.5 21.4 %reduce-scatter.2.cloned.1.call-done = f32[256,64]{0,1:T(8,128)} async-done(((f32[256,256]{0,1:T(8,128)}), f32[256,64]{0,1:T(8,128)}) %reduce-scatter.2.cloned.1.call-update) | async-done | bytes 65552 | tf_op jit(solution)/shard_map/reduce_scatter | solution.py:96
  217.9 1.7 fusion.4
  (44 shorter events, 3.2 us)
Async XLA Ops:
  6.5 48.5 %all-gather.3.cloned.1.call-start = ((), (), s32[]{:S(2)}) async-start(), calls=%async_computation.2 | async-start | bytes 1179648 | tf_op jit(solution)/shard_map/all_gather | solution.py:57
  65.4 5.7 %copy-start = (f32[32,8,128,128]{3,2,1,0:T(8,128)}, f32[32,8,128,128]{3,2,1,0:T(8,128)S(1)}, u32[]{:S(2)}) copy-start(f32[32,8,128,128]{3,2,1,0:T(8,128)S(1)} %copy.74) | copy-start | bytes 50331652
  114.5 5.7 %copy-start.1 = (f32[32,8,128,128]{3,2,1,0:T(8,128)}, f32[32,8,128,128]{3,2,1,0:T(8,128)S(1)}, u32[]{:S(2)}) copy-start(f32[32,8,128,128]{3,2,1,0:T(8,128)S(1)} %copy.77) | copy-start | bytes 50331652
  147.6 15.1 %copy-start.4 = (s32[2,3]{1,0:T(2,128)S(1)}, s32[2,3]{1,0:T(2,128)}, u32[]{:S(2)}) copy-start(s32[2,3]{1,0:T(2,128)} %param.5) | copy-start | bytes 76
  147.6 48.4 %copy-start.2 = (bf16[2048,256]{0,1:T(8,128)(2,1)S(1)}, bf16[2048,256]{0,1:T(8,128)(2,1)}, u32[]{:S(2)}) copy-start(bf16[2048,256]{0,1:T(8,128)(2,1)} %all-gather.3.cloned.1.call-done) | copy-start | bytes 3145732
  147.6 70.3 %copy-start.3 = (bf16[256,256]{0,1:T(8,128)(2,1)S(1)}, bf16[256,256]{0,1:T(8,128)(2,1)}, u32[]{:S(2)}) copy-start(bf16[256,256]{0,1:T(8,128)(2,1)} %all_gather.9) | copy-start | bytes 393220
  159.0 35.2 %all-to-all-start = ((f32[8,128,256]{2,1,0:T(8,128)}), f32[8,128,256]{2,1,0:T(8,128)S(1)}, u32[]{:S(2)}, u32[]{:S(2)}) async-start(f32[8,128,256]{2,1,0:T(8,128)} %copy.25), calls=%async_computation | async-start | bytes 2097152 | tf_op jit(solution)/shard_map/all_to_all | solution.py:90
  162.6 55.3 %reduce-scatter.2.cloned.1.call-start = ((), (), s32[]{:S(2)}) async-start(), calls=%async_computation.3 | async-start | bytes 327680 | tf_op jit(solution)/shard_map/reduce_scatter | solution.py:96
Sparse Core Ops, SparseCore 0:
  15.0 39.9 all-gather.2
  196.1 21.7 reduce-scatter.1
where the time goes:
time: 227 us; the launch traced here: 226 us
  local copies, waits for them, and re-layouts  47.9 us (21%)
  other arithmetic  45.2 us (20%)
  waiting for transfers between devices  40.2 us (18%)
  blocking collectives  39.4 us (17%)
  between operations  25.7 us (11%)
  matrix products  24.4 us (11%)
  starting transfers between devices  3.6 us (2%)
    unnamed x7, other arithmetic  44.1 us
    unnamed x19, local copies, waits for them, and re-layouts  33.5 us
    all_gather x1, blocking collectives, shards(): listed_back = lax.all_gather(triples, 'blk', axis=0, tiled=True)  31 us
    reduce_scatter x1, waiting for transfers between devices, shards(): owned_sum = lax.psum_scatter(owned, 'rep', scatter_dimension=1, tiled=True)  21.4 us
    all_gather x1, waiting for transfers between devices, shards(): gathered = lax.all_gather(own_rows, 'blk', axis=0, tiled=True)  18.7 us
    dot_general x2, matrix products, contract(): lax.dot_general(block.reshape(edge_size, edge_size * edge_size), upper, (...  11.6 us
    dot_general x2, matrix products, contract(): jnp.dot(block.reshape(edge_size * edge_size, edge_size), lower, preferred...  9.13 us
    all_gather x1, blocking collectives, shards(): own_rows = lax.all_gather(factor, 'rep', axis=1, tiled=True)  8.32 us
  transfers between devices with their start and end apart: 3, of which 2 were waited for; matrix products, arithmetic and copies ran while one was open for 5% of the time, Pallas kernels for 0%

commit v1 on v0

v1 whole, which is shorter than its diff:
```python
import functools

import jax
import jax.numpy as jnp
from jax import lax
from jax.experimental import pallas as pl
from jax.experimental.pallas import tpu as pltpu
from jax.sharding import PartitionSpec as P


def side_weights(triples):
    first_idx = triples[:, 0]
    second_idx = triples[:, 1]
    third_idx = triples[:, 2]
    same_upper = first_idx == second_idx
    same_lower = second_idx == third_idx
    apart = jnp.logical_and(jnp.logical_not(same_upper), jnp.logical_not(same_lower))
    every = jnp.logical_and(same_upper, same_lower)
    base = jnp.where(apart, 2.0, 1.0).astype(jnp.float32)
    dropped = jnp.where(every, 0.0, base)
    return jnp.stack([base, dropped, dropped], axis=1)


def contract_kernel(chunk, group, per_owner, trip_ref, w_ref, tab_ref, x_ref, out_ref, fi, fj, y1, y2, y3):
    s = pl.program_id(0)
    step = pl.program_id(1)
    i = trip_ref[s, 0]
    j = trip_ref[s, 1]
    k = trip_ref[s, 2]

    @pl.when(jnp.logical_and(s == 0, step == 0))
    def _():
        out_ref[...] = jnp.zeros_like(out_ref)

    @pl.when(step == 0)
    def _():
        fi[...] = tab_ref[i].astype(jnp.float32)
        fj[...] = tab_ref[j].astype(jnp.float32)
        y2[...] = jnp.zeros_like(y2)
        y3[...] = jnp.zeros_like(y3)

    middle = tab_ref[j]
    lower = tab_ref[k]

    @pl.loop(0, chunk // group)
    def _(g):
        start = pl.multiple_of(step * chunk + g * group, group)
        scale = fi[pl.ds(start, group), :]
        rows = []
        second = y2[...]
        third = y3[...]
        for u in range(group):
            block = x_ref[0, g * group + u]
            left = jnp.dot(block, lower, preferred_element_type=jnp.float32)
            right = lax.dot_general(
                block, middle, (((0,), (0,)), ((), ())), preferred_element_type=jnp.float32
            )
            line = scale[u : u + 1, :]
            second = second + left * line
            third = third + right * line
            rows.append(jnp.sum(left * fj[...], axis=0, keepdims=True))
        y2[...] = second
        y3[...] = third
        y1[pl.ds(start, group), :] = jnp.concatenate(rows, axis=0)

    @pl.when(step == pl.num_programs(1) - 1)
    def _():
        out_ref[i // per_owner] += w_ref[s, 0] * y1[...]
        out_ref[j // per_owner] += w_ref[s, 1] * y2[...]
        out_ref[k // per_owner] += w_ref[s, 2] * y3[...]


def contract_all(triples, weights, table, tensor_blocks, owner_count, per_owner):
    slots, edge = tensor_blocks.shape[:2]
    rank = table.shape[2]
    chunk = 32
    group = 8
    wide = pltpu.VMEM((edge, rank), jnp.float32)
    return pl.pallas_call(
        functools.partial(contract_kernel, chunk, group, per_owner),
        grid=(slots, edge // chunk),
        out_shape=jax.ShapeDtypeStruct((owner_count, edge, rank), jnp.float32),
        in_specs=[
            pl.BlockSpec(memory_space=pltpu.SMEM),
            pl.BlockSpec(memory_space=pltpu.SMEM),
            pl.BlockSpec(memory_space=pltpu.VMEM),
            pl.BlockSpec((1, chunk, edge, edge), lambda s, t: (s, t, 0, 0)),
        ],
        out_specs=pl.BlockSpec(memory_space=pltpu.VMEM),
        scratch_shapes=[wide] * 5,
        compiler_params=pltpu.CompilerParams(vmem_limit_bytes=40 * 1024 * 1024),
    )(triples, weights, table, tensor_blocks)


def owned_table(listed, owner_count, per_owner):
    myself = lax.axis_index("blk")
    flat = listed.reshape(owner_count, -1)
    mine = flat // per_owner == myself
    local = flat % per_owner
    column_ids = jnp.arange(per_owner, dtype=jnp.int32)
    hits = jnp.logical_and(mine[:, :, None], local[:, :, None] == column_ids[None, None, :])
    return jnp.any(hits, axis=1)


def shards(tensor_blocks, triples, slot_count, factor):
    own_rows = lax.all_gather(factor, "rep", axis=1, tiled=True)
    listed_back = lax.all_gather(triples, "blk", axis=0, tiled=True)
    block_size = tensor_blocks.shape[1]
    rank_width = own_rows.shape[1]
    owner_count = lax.axis_size("blk")
    per_owner = own_rows.shape[0] // block_size
    block_count = owner_count * per_owner
    gathered = lax.all_gather(own_rows, "blk", axis=0, tiled=True)
    gathered, listed_back = lax.optimization_barrier((gathered, listed_back))
    table = gathered.reshape(block_count, block_size, rank_width)
    slot_total = tensor_blocks.shape[0]
    alive = (jnp.arange(slot_total, dtype=jnp.int32) < slot_count[0]).astype(jnp.float32)
    weights = side_weights(triples) * alive[:, None]
    outgoing_sums = contract_all(triples, weights, table, tensor_blocks, owner_count, per_owner)
    arrived = lax.all_to_all(outgoing_sums, "blk", split_axis=0, concat_axis=0, tiled=True)
    gram_matrix = lax.dot_general(
        gathered, gathered, (((0,), (0,)), ((), ())), preferred_element_type=jnp.float32
    )
    hadamard = gram_matrix * gram_matrix
    column_width = factor.shape[1]
    column_start = lax.axis_index("rep") * column_width
    hadamard_cols = lax.dynamic_slice_in_dim(hadamard, column_start, column_width, 1)
    fitted = jnp.dot(
        own_rows.astype(jnp.float32),
        hadamard_cols,
        preferred_element_type=jnp.float32,
        precision=lax.Precision.HIGHEST,
    )
    placing = owned_table(listed_back, owner_count, per_owner).astype(jnp.float32)
    owned = jnp.einsum("ql,qar->lar", placing, arrived, precision=lax.Precision.HIGHEST).reshape(
        per_owner * block_size, rank_width
    )
    owned_sum = lax.psum_scatter(owned, "rep", scatter_dimension=1, tiled=True)
    return fitted - owned_sum


def solution(mesh):
    in_specs = (
        P(("blk", "rep"), None, None, None),
        P(("blk", "rep"), None),
        P(("blk", "rep")),
        P("blk", "rep"),
    )
    out_specs = P("blk", "rep")
    return jax.shard_map(shards, mesh=mesh, in_specs=in_specs, out_specs=out_specs, check_vma=False)
```

time: 227 us -> 137 us (0.60)
  other arithmetic: 45.2 us -> 1.12 us
  local copies, waits for them, and re-layouts: 47.9 us -> 6.9 us
  matrix products: 24.4 us -> 2.74 us
  waiting for transfers between devices: 40.2 us -> 61.4 us
  Pallas kernels: 0 us -> 16.9 us
  between operations: 25.7 us -> 14.1 us
  blocking collectives: 39.4 us -> 29.4 us
    unnamed x7 -> x0, other arithmetic: 44.1 us -> none
    unnamed x19 -> x9, local copies, waits for them, and re-layouts: 33.5 us -> 4.78 us
    all_to_all x1, waiting for transfers between devices: 0.01 us -> 25.1 us  [shards(): lax.all_to_all(outgoing_sums, 'blk', split_axis=0, concat_axis=0, tiled=T...]
    dot_general x5 -> x0, matrix products: 21.7 us -> none  [the longest x2 11.6 us: contract(): lax.dot_general(block.reshape(edge_size, edge_size * edge_size), upper, (...]
    pallas_call x0 -> x1, Pallas kernels: none -> 16.9 us  [contract_all(): pl.pallas_call(functools.partial(contract_kernel, chunk, group, per_owner...]
    all_gather x1, blocking collectives: 31 us -> 21.1 us  [shards(): listed_back = lax.all_gather(triples, 'blk', axis=0, tiled=True)]
    slice x2 -> x0, local copies, waits for them, and re-layouts: 7.61 us -> none  [the longest x1 6.05 us: shards(): results.extend(contract(tensor_blocks[slot_index], upper, middle, lower))]
    reduce_scatter x1, waiting for transfers between devices: 21.4 us -> 18.7 us  [shards(): owned_sum = lax.psum_scatter(owned, 'rep', scatter_dimension=1, tiled=True)]
  transfers between devices with their start and end apart: 3 -> 3, of which waited for: 2 -> 3; matrix products, arithmetic and copies ran while one was open for 5% -> 1% of each run, Pallas kernels for 0% -> 0%
where the time goes in v1:
time: 137 us; the launch traced here: 136 us
  waiting for transfers between devices  61.4 us (45%)
  blocking collectives  29.4 us (21%)
  Pallas kernels  16.9 us (12%)
  between operations  14.1 us (10%)
  local copies, waits for them, and re-layouts  6.9 us (5%)
  starting transfers between devices  3.6 us (3%)
  matrix products  2.74 us (2%)
    all_to_all x1, waiting for transfers between devices, shards(): lax.all_to_all(outgoing_sums, 'blk', split_axis=0, concat_axis=0, tiled=T...  25.1 us
    all_gather x1, blocking collectives, shards(): listed_back = lax.all_gather(triples, 'blk', axis=0, tiled=True)  21.1 us
    reduce_scatter x1, waiting for transfers between devices, shards(): owned_sum = lax.psum_scatter(owned, 'rep', scatter_dimension=1, tiled=True)  18.7 us
    all_gather x1, waiting for transfers between devices, shards(): gathered = lax.all_gather(own_rows, 'blk', axis=0, tiled=True)  17.4 us
    pallas_call x1, Pallas kernels, contract_all(): pl.pallas_call(functools.partial(contract_kernel, chunk, group, per_owner...  16.9 us
    all_gather x1, blocking collectives, shards(): own_rows = lax.all_gather(factor, 'rep', axis=1, tiled=True)  8.33 us
    unnamed x9, local copies, waits for them, and re-layouts  4.78 us
    all_to_all x1, starting transfers between devices, shards(): lax.all_to_all(outgoing_sums, 'blk', split_axis=0, concat_axis=0, tiled=T...  3.56 us
  transfers between devices with their start and end apart: 3, of which 3 were waited for; matrix products, arithmetic and copies ran while one was open for 1% of the time, Pallas kernels for 0%

profile of v1, /device:TPU:0, one launch (start us, length us, event | category | flops | bytes accessed | tf_op | source)
XLA Modules:
  0.0 136.1 jit_solution(9320856892472648409)
XLA Ops:
  6.5 0.0 all-gather.3.cloned.1.call-start
  6.5 8.3 %all_gather.9 = bf16[256,256]{0,1:T(8,128)(2,1)} all-gather(bf16[256,64]{0,1:T(8,128)(2,1)} %param.7), channel_id=1, replica_groups=mesh['blk'=8,'rep'=4] {'rep'}, dimensions={1}, use_global_device_ids=true | all-gather | bytes 163840 | tf_op jit(solution)/shard_map/all_gather | solution.py:106
  14.9 0.0 all-gather.3.cloned.1.call-update
  15.5 21.1 %all-gather = s32[8,2,3]{2,1,0:T(2,128)S(1)} all-gather(s32[1,2,3]{2,1,0:T(2,128)} %bitcast.23), channel_id=1, replica_groups=mesh['blk'=8,'rep'=4] {'blk'}, dimensions={0}, use_global_device_ids=true | all-gather | bytes 216 | tf_op jit(solution)/shard_map/all_gather | solution.py:107
  36.6 0.1 copy.27
  36.7 0.9 and_select_fusion.1
  37.6 0.1 maximum_multiply_fusion.w_ref
  37.6 17.4 %all-gather.3.cloned.1.call-done = bf16[2048,256]{0,1:T(8,128)(2,1)} async-done(((bf16[256,256]{0,1:T(8,128)(2,1)}), bf16[2048,256]{0,1:T(8,128)(2,1)}) %all-gather.3.cloned.1.call-update) | async-done | bytes 1048592 | tf_op jit(solution)/shard_map/all_gather | solution.py:113
  55.1 1.5 %copy.22 = bf16[2048,256]{1,0:T(8,128)(2,1)S(1)} copy(bf16[2048,256]{0,1:T(8,128)(2,1)} %all-gather.3.cloned.1.call-done) | data formatting | bytes 2097152 | tf_op jit(solution)/shard_map/optimization_barrier | solution.py:114
  56.5 0.0 copy-start
  56.6 3.4 %copy-done = bf16[2,128,128,128]{3,2,1,0:T(8,128)(2,1)S(1)} copy-done((bf16[2,128,128,128]{3,2,1,0:T(8,128)(2,1)S(1)}, bf16[2,128,128,128]{3,2,1,0:T(8,128)(2,1)}, u32[]{:S(2)}) %copy-start) | copy-done | bytes 8388632
  59.9 0.0 copy-start.1
  59.9 0.7 copy-done.1
  60.6 0.0 copy-start.2
  60.6 0.0 copy-start.3
  60.6 16.9 %shard_map.46 = f32[8,128,256]{2,1,0:T(8,128)} custom-call(s32[2,3]{1,0:T(2,128)S(1)} %copy-done.1, f32[2,3]{1,0:T(2,128)S(1)} %maximum_multiply_fusion.w_ref, bf16[16,128,256]{2,1,0:T(8,128)(2,1)S(1)} %bitcast.22, bf16[2,128,128,128]{3,2,1,0:T(8,128)(2,1)S(1)} %copy-done), custom_call_target="tpu_custom_call" | custom-call | tf_op jit(solution)/shard_map/pallas_call | solution.py:79
  77.5 3.6 %all-to-all-start = ((f32[8,128,256]{2,1,0:T(8,128)}), f32[8,128,256]{2,1,0:T(8,128)S(1)}, u32[]{:S(2)}, u32[]{:S(2)}) async-start(f32[8,128,256]{2,1,0:T(8,128)} %shard_map.46), calls=%async_computation | async-start | bytes 2097152 | tf_op jit(solution)/shard_map/all_to_all | solution.py:120
  81.1 0.0 reduce-scatter.2.cloned.1.call-start
  81.1 0.1 copy.21
  81.2 0.1 reshape.64
  81.3 0.1 fusion.2
  81.5 25.1 %all-to-all-done = f32[8,128,256]{2,1,0:T(8,128)S(1)} async-done(((f32[8,128,256]{2,1,0:T(8,128)}), f32[8,128,256]{2,1,0:T(8,128)S(1)}, u32[]{:S(2)}, u32[]{:S(2)}) %all-to-all-start) | async-done | bytes 1048608 | tf_op jit(solution)/shard_map/all_to_all | solution.py:120
  106.6 0.4 copy.25
  107.0 0.6 fusion.6
  107.6 0.7 copy.31
  108.3 0.0 reduce-scatter.2.cloned.1.call-update
  108.4 0.0 copy-done.2
  108.4 0.5 fusion.9
  108.9 18.7 %reduce-scatter.2.cloned.1.call-done = f32[256,64]{0,1:T(8,128)} async-done(((f32[256,256]{0,1:T(8,128)}), f32[256,64]{0,1:T(8,128)}) %reduce-scatter.2.cloned.1.call-update) | async-done | bytes 65552 | tf_op jit(solution)/shard_map/reduce_scatter | solution.py:138
  127.6 0.0 copy-done.3
  127.6 1.7 %fusion = f32[256,64]{0,1:T(8,128)} fusion(f32[256,64]{0,1:T(8,128)} %reduce-scatter.2.cloned.1.call-done, bf16[256,256]{0,1:T(8,128)(2,1)S(1)} %copy-done.3, f32[256,256]{0,1:T(8,128)S(1)} %fusion.9, s32[]{:T(128)S(6)} %select_n.34), kind=kOutput, calls=%fused_computation.1 | convolution fusion | flops 50364416 | bytes 327684 | tf_op jit(solution)/shard_map/dot_general | solution.py:128
  (4 shorter events, 0.0 us)
Async XLA Ops:
  6.5 48.5 %all-gather.3.cloned.1.call-start = ((), (), s32[]{:S(2)}) async-start(), calls=%async_computation.2 | async-start | bytes 1179648 | tf_op jit(solution)/shard_map/all_gather | solution.py:113
  56.5 3.4 %copy-start = (bf16[2,128,128,128]{3,2,1,0:T(8,128)(2,1)S(1)}, bf16[2,128,128,128]{3,2,1,0:T(8,128)(2,1)}, u32[]{:S(2)}) copy-start(bf16[2,128,128,128]{3,2,1,0:T(8,128)(2,1)} %x_ref.1) | copy-start | bytes 25165828
  59.9 0.7 copy-start.1
  60.6 47.8 %copy-start.2 = (bf16[2048,256]{0,1:T(8,128)(2,1)S(1)}, bf16[2048,256]{0,1:T(8,128)(2,1)}, u32[]{:S(2)}) copy-start(bf16[2048,256]{0,1:T(8,128)(2,1)} %all-gather.3.cloned.1.call-done) | copy-start | bytes 3145732
  60.6 67.0 %copy-start.3 = (bf16[256,256]{0,1:T(8,128)(2,1)S(1)}, bf16[256,256]{0,1:T(8,128)(2,1)}, u32[]{:S(2)}) copy-start(bf16[256,256]{0,1:T(8,128)(2,1)} %all_gather.9) | copy-start | bytes 393220
  77.5 29.1 %all-to-all-start = ((f32[8,128,256]{2,1,0:T(8,128)}), f32[8,128,256]{2,1,0:T(8,128)S(1)}, u32[]{:S(2)}, u32[]{:S(2)}) async-start(f32[8,128,256]{2,1,0:T(8,128)} %shard_map.46), calls=%async_computation | async-start | bytes 2097152 | tf_op jit(solution)/shard_map/all_to_all | solution.py:120
  81.1 46.5 %reduce-scatter.2.cloned.1.call-start = ((), (), s32[]{:S(2)}) async-start(), calls=%async_computation.3 | async-start | bytes 327680 | tf_op jit(solution)/shard_map/reduce_scatter | solution.py:138
Sparse Core Ops, SparseCore 0:
  15.0 40.0 all-gather.2
  108.5 19.0 reduce-scatter.1

commit v2 on v1

v2 whole, which is shorter than its diff:
```python
import functools

import jax
import jax.numpy as jnp
from jax import lax
from jax.experimental import pallas as pl
from jax.experimental.pallas import tpu as pltpu
from jax.sharding import PartitionSpec as P


def side_weights(triples):
    first_idx = triples[:, 0]
    second_idx = triples[:, 1]
    third_idx = triples[:, 2]
    same_upper = first_idx == second_idx
    same_lower = second_idx == third_idx
    apart = jnp.logical_and(jnp.logical_not(same_upper), jnp.logical_not(same_lower))
    every = jnp.logical_and(same_upper, same_lower)
    base = jnp.where(apart, 2.0, 1.0).astype(jnp.float32)
    dropped = jnp.where(every, 0.0, base)
    return jnp.stack([base, dropped, dropped], axis=1)


MESH = pl.DeviceIdType.MESH


def bits_of(size):
    return [1 << p for p in range(size.bit_length() - 1)]


def flip(index, bit):
    return index + bit - 2 * bit * ((index // bit) % 2)


def place(rep, blk, combo):
    for (axis, bit), on in combo:
        if on:
            if axis == "rep":
                rep = flip(rep, bit)
            else:
                blk = flip(blk, bit)
    return rep, blk


def combos(steps):
    found = [()]
    for step in steps:
        found = [c + ((step, on),) for c in found for on in (1, 0)]
    return found


def greet(steps, rep, blk):
    barrier = pltpu.get_barrier_semaphore()
    for step in steps:
        to_rep, to_blk = place(rep, blk, ((step, 1),))
        pl.semaphore_signal(barrier, inc=1, device_id=(to_blk, to_rep), device_id_type=MESH)
    pl.semaphore_wait(barrier, len(steps))


def gather_kernel(steps, own_ref, all_ref, send_sem, recv_sem):
    rep = lax.axis_index("rep")
    blk = lax.axis_index("blk")
    greet(steps, rep, blk)
    all_ref[rep, blk] = own_ref[...]
    sent = []

    def copy(at, combo, index):
        src_rep, src_blk = place(rep, blk, combo)
        to_rep, to_blk = place(rep, blk, ((steps[at], 1),))
        where = all_ref.at[src_rep, src_blk]
        return pltpu.make_async_remote_copy(
            src_ref=where,
            dst_ref=where,
            send_sem=send_sem.at[at, index],
            recv_sem=recv_sem.at[at, index],
            device_id=(to_blk, to_rep),
            device_id_type=MESH,
        )

    def spread(first, combo):
        for at in range(first, len(steps)):
            full = combo + tuple((s, 0) for s in steps[len(combo):at])
            out = copy(at, full, combos(steps[:at])[::-1].index(full))
            out.start()
            sent.append(out)

    spread(0, ())
    for at in range(len(steps)):
        for index, combo in enumerate(combos(steps[:at])[::-1]):
            mine = combo + ((steps[at], 1),)
            copy(at, mine, index).wait_recv()
            spread(at + 1, mine)
    for out in sent:
        out.wait_send()


def reduce_kernel(steps, part_ref, out_ref, acc, land, send_sem, recv_sem):
    rep = lax.axis_index("rep")
    blk = lax.axis_index("blk")
    greet(steps, rep, blk)
    base = [0]
    for at in range(len(steps)):
        base.append(base[-1] + (1 << (len(steps) - 1 - at)))

    def copy(at, combo, index):
        src_rep, src_blk = place(rep, blk, ((steps[at], 1),) + combo)
        to_rep, to_blk = place(rep, blk, ((steps[at], 1),))
        slot = base[at] + index
        source = part_ref if at == 0 else acc
        return pltpu.make_async_remote_copy(
            src_ref=source.at[src_rep, src_blk],
            dst_ref=land.at[slot],
            send_sem=send_sem.at[slot],
            recv_sem=recv_sem.at[slot],
            device_id=(to_blk, to_rep),
            device_id_type=MESH,
        )

    sent = []
    for index, combo in enumerate(combos(steps[1:])):
        out = copy(0, combo, index)
        out.start()
        sent.append(out)
    for at in range(len(steps)):
        later = combos(steps[at + 2:])
        for index, combo in enumerate(combos(steps[at + 1:])):
            copy(at, combo, index).wait_recv()
            at_rep, at_blk = place(rep, blk, combo)
            held = part_ref if at == 0 else acc
            total = held[at_rep, at_blk] + land[base[at] + index]
            if at == len(steps) - 1:
                out_ref[...] = total
            else:
                acc[at_rep, at_blk] = total
                if combo[0][1]:
                    out = copy(at + 1, combo[1:], later.index(combo[1:]))
                    out.start()
                    sent.append(out)
    for out in sent:
        out.wait_send()


def gather_all(own, rep_count, blk_count):
    steps = [("blk", b) for b in bits_of(blk_count)[::-1]] + [("rep", b) for b in bits_of(rep_count)[::-1]]
    most = max(1, rep_count * blk_count // 2)
    return pl.pallas_call(
        functools.partial(gather_kernel, steps),
        out_shape=jax.ShapeDtypeStruct((rep_count, blk_count) + own.shape, own.dtype),
        in_specs=[pl.BlockSpec(memory_space=pltpu.VMEM)],
        out_specs=pl.BlockSpec(memory_space=pltpu.VMEM),
        scratch_shapes=[
            pltpu.SemaphoreType.DMA((len(steps), most)),
            pltpu.SemaphoreType.DMA((len(steps), most)),
        ],
        compiler_params=pltpu.CompilerParams(
            collective_id=0, has_side_effects=True, vmem_limit_bytes=40 * 1024 * 1024
        ),
    )(own)


def reduce_all(parts):
    rep_count, blk_count = parts.shape[:2]
    steps = [("rep", b) for b in bits_of(rep_count)] + [("blk", b) for b in bits_of(blk_count)]
    total = rep_count * blk_count - 1
    piece = parts.shape[2:]
    return pl.pallas_call(
        functools.partial(reduce_kernel, steps),
        out_shape=jax.ShapeDtypeStruct(piece, parts.dtype),
        in_specs=[pl.BlockSpec(memory_space=pltpu.VMEM)],
        out_specs=pl.BlockSpec(memory_space=pltpu.VMEM),
        scratch_shapes=[
            pltpu.VMEM(parts.shape, parts.dtype),
            pltpu.VMEM((total,) + piece, parts.dtype),
            pltpu.SemaphoreType.DMA((total,)),
            pltpu.SemaphoreType.DMA((total,)),
        ],
        compiler_params=pltpu.CompilerParams(
            collective_id=1, has_side_effects=True, vmem_limit_bytes=48 * 1024 * 1024
        ),
    )(parts)


def contract_kernel(
    chunk, group, per_owner, cols, trip_ref, w_ref, tab_ref, x_ref, out_ref, fi, fj, fk, y1, y2, y3
):
    s = pl.program_id(0)
    step = pl.program_id(1)
    depth, lanes = tab_ref.shape[2:]
    edge, rank = fi.shape
    fold = lanes // cols
    groups = edge // depth
    lane_group = lax.broadcasted_iota(jnp.int32, (depth, lanes), 1) // cols

    def load_block(index, dest):
        owner = index // per_owner
        for u in range(groups):
            g = (index % per_owner) * groups + u
            for h in range(rank // lanes):
                tile = jnp.zeros((depth, lanes), jnp.float32)
                for m in range(fold):
                    piece = tab_ref[h * fold + m, owner].astype(jnp.float32)
                    moved = pltpu.roll(piece, ((m + fold - g) % fold) * cols, 1)
                    tile = jnp.where(lane_group == m, moved, tile)
                dest[u * depth : (u + 1) * depth, h * lanes : (h + 1) * lanes] = tile.astype(dest.dtype)

    def add_block(index, weight, value):
        owner = index // per_owner
        for u in range(groups):
            g = (index % per_owner) * groups + u
            for h in range(rank // lanes):
                tile = weight * value[u * depth : (u + 1) * depth, h * lanes : (h + 1) * lanes]
                for m in range(fold):
                    moved = pltpu.roll(tile, ((g + fold - m) % fold) * cols, 1)
                    out_ref[h * fold + m, owner] += jnp.where(lane_group == g, moved, 0.0)

    i = trip_ref[s, 0]
    j = trip_ref[s, 1]
    k = trip_ref[s, 2]

    @pl.when(jnp.logical_and(s == 0, step == 0))
    def _():
        out_ref[...] = jnp.zeros_like(out_ref)

    @pl.when(step == 0)
    def _():
        load_block(i, fi)
        load_block(j, fj)
        load_block(k, fk)
        y2[...] = jnp.zeros_like(y2)
        y3[...] = jnp.zeros_like(y3)

    middle = fj[...].astype(jnp.bfloat16)
    lower = fk[...].astype(jnp.bfloat16)

    @pl.loop(0, chunk // group)
    def _(g):
        start = pl.multiple_of(step * chunk + g * group, group)
        scale = fi[pl.ds(start, group), :]
        rows = []
        second = y2[...]
        third = y3[...]
        for u in range(group):
            block = x_ref[0, g * group + u]
            left = jnp.dot(block, lower, preferred_element_type=jnp.float32)
            right = lax.dot_general(
                block, middle, (((0,), (0,)), ((), ())), preferred_element_type=jnp.float32
            )
            line = scale[u : u + 1, :]
            second = second + left * line
            third = third + right * line
            rows.append(jnp.sum(left * fj[...], axis=0, keepdims=True))
        y2[...] = second
        y3[...] = third
        y1[pl.ds(start, group), :] = jnp.concatenate(rows, axis=0)

    @pl.when(step == pl.num_programs(1) - 1)
    def _():
        add_block(i, w_ref[s, 0], y1)
        add_block(j, w_ref[s, 1], y2)
        add_block(k, w_ref[s, 2], y3)


def contract_all(triples, weights, table, tensor_blocks, per_owner, cols, rank):
    slots, edge = tensor_blocks.shape[:2]
    chunk = 32
    group = 8
    wide = pltpu.VMEM((edge, rank), jnp.float32)
    return pl.pallas_call(
        functools.partial(contract_kernel, chunk, group, per_owner, cols),
        grid=(slots, edge // chunk),
        out_shape=jax.ShapeDtypeStruct(table.shape, jnp.float32),
        in_specs=[
            pl.BlockSpec(memory_space=pltpu.SMEM),
            pl.BlockSpec(memory_space=pltpu.SMEM),
            pl.BlockSpec(memory_space=pltpu.VMEM),
            pl.BlockSpec((1, chunk, edge, edge), lambda s, t: (s, t, 0, 0)),
        ],
        out_specs=pl.BlockSpec(memory_space=pltpu.VMEM),
        scratch_shapes=[wide] * 6,
        compiler_params=pltpu.CompilerParams(vmem_limit_bytes=48 * 1024 * 1024),
    )(triples, weights, table, tensor_blocks)


def shards(tensor_blocks, triples, slot_count, factor):
    rows, cols = factor.shape
    edge = tensor_blocks.shape[1]
    rep_count = lax.axis_size("rep")
    blk_count = lax.axis_size("blk")
    rank = cols * rep_count
    fold = 128 // cols
    depth = rows // fold
    packed = factor.reshape(fold, depth, cols).transpose(1, 0, 2).reshape(depth, fold * cols)
    table = gather_all(packed, rep_count, blk_count)
    slot_total = tensor_blocks.shape[0]
    alive = (jnp.arange(slot_total, dtype=jnp.int32) < slot_count[0]).astype(jnp.float32)
    weights = side_weights(triples) * alive[:, None]
    parts = contract_all(triples, weights, table, tensor_blocks, rows // edge, cols, rank)
    moment = reduce_all(parts)
    moment = moment.reshape(depth, fold, cols).transpose(1, 0, 2).reshape(rows, cols)

    flat = table.reshape(rep_count, blk_count * depth, fold * cols)
    mine = lax.dynamic_index_in_dim(flat, lax.axis_index("rep"), 0, keepdims=False)
    pairs = lax.dot_general(
        flat, mine, (((1,), (0,)), ((), ())), preferred_element_type=jnp.float32
    )
    gram_cols = sum(
        pairs[:, g * cols : (g + 1) * cols, g * cols : (g + 1) * cols] for g in range(fold)
    ).reshape(rank, cols)
    own = lax.dynamic_index_in_dim(table, lax.axis_index("blk"), 1, keepdims=False)
    own_rows = own.reshape(rep_count, depth, fold, cols).transpose(2, 1, 0, 3).reshape(rows, rank)
    fitted = jnp.dot(
        own_rows.astype(jnp.float32),
        gram_cols * gram_cols,
        preferred_element_type=jnp.float32,
        precision=lax.Precision.HIGHEST,
    )
    return fitted - moment


def solution(mesh):
    in_specs = (
        P(("blk", "rep"), None, None, None),
        P(("blk", "rep"), None),
        P(("blk", "rep")),
        P("blk", "rep"),
    )
    out_specs = P("blk", "rep")
    return jax.shard_map(shards, mesh=mesh, in_specs=in_specs, out_specs=out_specs, check_vma=False)
```

time: 137 us -> 66.3 us (0.48)
  waiting for transfers between devices: 61.4 us -> 0 us
  Pallas kernels: 16.9 us -> 60.9 us
  blocking collectives: 29.4 us -> 0 us
  between operations: 14.1 us -> 0.75 us
  local copies, waits for them, and re-layouts: 6.9 us -> 2.18 us
  starting transfers between devices: 3.6 us -> 0 us
  matrix products: 2.74 us -> 1.18 us
    pallas_call x0 -> x2, Pallas kernels: none -> 43.4 us  [the longest x1 24.3 us: reduce_all(): pl.pallas_call(functools.partial(reduce_kernel, steps), out_shape=jax.Sha...]
    all_gather x2 -> x0, blocking collectives: 29.4 us -> none  [the longest x1 21.1 us: shards(): listed_back = lax.all_gather(triples, 'blk', axis=0, tiled=True)]
    all_to_all x1 -> x0, waiting for transfers between devices: 25.1 us -> none  [shards(): lax.all_to_all(outgoing_sums, 'blk', split_axis=0, concat_axis=0, tiled=T...]
    reduce_scatter x1 -> x0, waiting for transfers between devices: 18.7 us -> none  [shards(): owned_sum = lax.psum_scatter(owned, 'rep', scatter_dimension=1, tiled=True)]
    all_gather x1 -> x0, waiting for transfers between devices: 17.4 us -> none  [shards(): gathered = lax.all_gather(own_rows, 'blk', axis=0, tiled=True)]
    unnamed x9 -> x2, local copies, waits for them, and re-layouts: 4.78 us -> 0.68 us
    all_to_all x1 -> x0, starting transfers between devices: 3.56 us -> none  [shards(): lax.all_to_all(outgoing_sums, 'blk', split_axis=0, concat_axis=0, tiled=T...]
    optimization_barrier x3 -> x0, local copies, waits for them, and re-layouts: 1.64 us -> none  [shards(): gathered, listed_back = lax.optimization_barrier((gathered, listed_back))]
  transfers between devices with their start and end apart: 3 -> 0, of which waited for: 3 -> 0; matrix products, arithmetic and copies ran while one was open for 1% -> 0% of each run, Pallas kernels for 0% -> 0%
where the time goes in v2:
time: 66.3 us; the launch traced here: 66 us
  Pallas kernels  60.9 us (92%)
  local copies, waits for them, and re-layouts  2.18 us (3%)
  matrix products  1.18 us (2%)
  other arithmetic  1.05 us (2%)
  between operations  0.75 us (1%)
    pallas_call x1, Pallas kernels, reduce_all(): pl.pallas_call(functools.partial(reduce_kernel, steps), out_shape=jax.Sha...  24.3 us
    pallas_call x1, Pallas kernels, gather_all(): pl.pallas_call(functools.partial(gather_kernel, steps), out_shape=jax.Sha...  19.1 us
    pallas_call x1, Pallas kernels, contract_all(): pl.pallas_call(functools.partial(contract_kernel, chunk, group, per_owner...  17.5 us

profile of v2, /device:TPU:0, one launch (start us, length us, event | category | flops | bytes accessed | tf_op | source)
XLA Modules:
  0.0 66.0 jit_solution(8938037603726599096)
XLA Ops:
  0.7 0.9 %and_select_fusion.1 = (f32[2,1]{1,0:T(2,128)S(1)}, pred[2,1]{1,0:T(4,128)(4,1)S(1)}, pred[2,1]{1,0:T(4,128)(4,1)S(1)}) fusion(s32[2,3]{1,0:T(2,128)} %trip_ref.1), kind=kLoop, calls=%fused_computation.10 | loop fusion | flops 12 | bytes 36 | tf_op jit(solution)/shard_map/jit(_where)/select_n | solution.py:19
  1.5 0.1 maximum_multiply_fusion.w_ref
  1.6 0.8 %reshape.29 = bf16[2,128,64]{1,0,2:T(2,128)(2,1)S(1)} reshape(bf16[256,64]{0,1:T(8,128)(2,1)} %param.7) | data formatting | bytes 65536 | tf_op jit(solution)/shard_map/reshape | solution.py:292
  2.4 0.1 copy.16.own_ref
  2.5 19.1 %shard_map.46.tab_ref = bf16[4,8,128,128]{3,2,1,0:T(8,128)(2,1)S(1)} custom-call(bf16[128,128]{1,0:T(8,128)(2,1)S(1)} %copy.16.own_ref), custom_call_target="tpu_custom_call" | custom-call | tf_op jit(solution)/shard_map/pallas_call | solution.py:146
  21.7 0.1 copy.17
  21.8 0.1 copy.18
  21.9 0.3 convolution_bitcast_fusion
  22.3 0.1 fusion.4
  22.4 0.1 copy.20
  22.5 0.1 mul.15
  22.6 0.0 copy-start
  22.6 0.7 %copy-done = s32[2,3]{1,0:T(2,128)S(1)} copy-done((s32[2,3]{1,0:T(2,128)S(1)}, s32[2,3]{1,0:T(2,128)}, u32[]{:S(2)}) %copy-start) | copy-done | bytes 48
  23.3 17.5 %shard_map.47.part_ref = f32[4,8,128,128]{3,2,1,0:T(8,128)S(1)} custom-call(s32[2,3]{1,0:T(2,128)S(1)} %copy-done, f32[2,3]{1,0:T(2,128)S(1)} %maximum_multiply_fusion.w_ref, bf16[4,8,128,128]{3,2,1,0:T(8,128)(2,1)S(1)} %shard_map.46.tab_ref, bf16[2,128,128,128]{3,2,1,0:T(8,128)(2,1)} %x_ref.1), custom_call_target="tpu_custom_call" | custom-call | tf_op jit(solution)/shard_map/pallas_call | solution.py:268
  40.8 24.3 %shard_map.48 = f32[128,128]{1,0:T(8,128)S(1)} custom-call(f32[4,8,128,128]{3,2,1,0:T(8,128)S(1)} %shard_map.47.part_ref), custom_call_target="tpu_custom_call" | custom-call | tf_op jit(solution)/shard_map/pallas_call | solution.py:166
  65.1 0.1 copy.21
  65.2 0.8 %convolution_subtract_fusion = f32[256,64]{0,1:T(8,128)} fusion(f32[256,64]{0,1:T(8,128)S(1)} %mul.15, bf16[32,8,2,128]{3,2,1,0:T(2,128)(2,1)S(1)} %bitcast.35, f32[2,8,8,128]{3,2,1,0:T(8,128)S(1)} %bitcast.37), kind=kOutput, calls=%fused_computation.1 | convolution fusion | flops 50348032 | bytes 327680 | tf_op jit(solution)/shard_map/dot_general | solution.py:311
  (4 shorter events, 0.0 us)
Async XLA Ops:
  22.6 0.7 %copy-start = (s32[2,3]{1,0:T(2,128)S(1)}, s32[2,3]{1,0:T(2,128)}, u32[]{:S(2)}) copy-start(s32[2,3]{1,0:T(2,128)} %trip_ref.1) | copy-start | bytes 76

commit v3 on v2

--- a/solution.py
+++ b/solution.py
@@ -6,19 +6,6 @@
 from jax.experimental import pallas as pl
 from jax.experimental.pallas import tpu as pltpu
 from jax.sharding import PartitionSpec as P
-
-
-def side_weights(triples):
-    first_idx = triples[:, 0]
-    second_idx = triples[:, 1]
-    third_idx = triples[:, 2]
-    same_upper = first_idx == second_idx
-    same_lower = second_idx == third_idx
-    apart = jnp.logical_and(jnp.logical_not(same_upper), jnp.logical_not(same_lower))
-    every = jnp.logical_and(same_upper, same_lower)
-    base = jnp.where(apart, 2.0, 1.0).astype(jnp.float32)
-    dropped = jnp.where(every, 0.0, base)
-    return jnp.stack([base, dropped, dropped], axis=1)
 
 
 MESH = pl.DeviceIdType.MESH
@@ -57,100 +44,115 @@
     pl.semaphore_wait(barrier, len(steps))
 
 
-def gather_kernel(steps, own_ref, all_ref, send_sem, recv_sem):
+def gather_kernel(orders, own_ref, all_ref, send_sem, recv_sem):
     rep = lax.axis_index("rep")
     blk = lax.axis_index("blk")
-    greet(steps, rep, blk)
+    greet(orders[0], rep, blk)
     all_ref[rep, blk] = own_ref[...]
+    share = own_ref.shape[0] // len(orders)
     sent = []
 
-    def copy(at, combo, index):
+    def copy(part, at, combo, index):
+        steps = orders[part]
         src_rep, src_blk = place(rep, blk, combo)
         to_rep, to_blk = place(rep, blk, ((steps[at], 1),))
-        where = all_ref.at[src_rep, src_blk]
+        where = all_ref.at[src_rep, src_blk, pl.ds(part * share, share)]
         return pltpu.make_async_remote_copy(
             src_ref=where,
             dst_ref=where,
-            send_sem=send_sem.at[at, index],
-            recv_sem=recv_sem.at[at, index],
+            send_sem=send_sem.at[part, (1 << at) - 1 + index],
+            recv_sem=recv_sem.at[part, (1 << at) - 1 + index],
             device_id=(to_blk, to_rep),
             device_id_type=MESH,
         )
 
-    def spread(first, combo):
+    def spread(part, first, combo):
+        steps = orders[part]
         for at in range(first, len(steps)):
             full = combo + tuple((s, 0) for s in steps[len(combo):at])
-            out = copy(at, full, combos(steps[:at])[::-1].index(full))
+            out = copy(part, at, full, combos(steps[:at])[::-1].index(full))
             out.start()
             sent.append(out)
 
-    spread(0, ())
-    for at in range(len(steps)):
-        for index, combo in enumerate(combos(steps[:at])[::-1]):
-            mine = combo + ((steps[at], 1),)
-            copy(at, mine, index).wait_recv()
-            spread(at + 1, mine)
+    for part in range(len(orders)):
+        spread(part, 0, ())
+    for at in range(len(orders[0])):
+        for index in range(1 << at):
+            for part, steps in enumerate(orders):
+                mine = combos(steps[:at])[::-1][index] + ((steps[at], 1),)
+                copy(part, at, mine, index).wait_recv()
+                spread(part, at + 1, mine)
     for out in sent:
         out.wait_send()
 
 
-def reduce_kernel(steps, part_ref, out_ref, acc, land, send_sem, recv_sem):
+def reduce_kernel(orders, part_ref, out_ref, acc, land, send_sem, recv_sem):
     rep = lax.axis_index("rep")
     blk = lax.axis_index("blk")
-    greet(steps, rep, blk)
+    greet(orders[0], rep, blk)
+    share = out_ref.shape[0] // len(orders)
+    count = len(orders[0])
     base = [0]
-    for at in range(len(steps)):
-        base.append(base[-1] + (1 << (len(steps) - 1 - at)))
-
-    def copy(at, combo, index):
-        src_rep, src_blk = place(rep, blk, ((steps[at], 1),) + combo)
-        to_rep, to_blk = place(rep, blk, ((steps[at], 1),))
+    for at in range(count):
+        base.append(base[-1] + (1 << (count - 1 - at)))
+
+    def copy(part, at, combo, index):
+        step = orders[part][at]
+        src_rep, src_blk = place(rep, blk, ((step, 1),) + combo)
+        to_rep, to_blk = place(rep, blk, ((step, 1),))
         slot = base[at] + index
         source = part_ref if at == 0 else acc
+        rows = pl.ds(part * share, share)
         return pltpu.make_async_remote_copy(
-            src_ref=source.at[src_rep, src_blk],
-            dst_ref=land.at[slot],
-            send_sem=send_sem.at[slot],
-            recv_sem=recv_sem.at[slot],
+            src_ref=source.at[src_rep, src_blk, rows],
+            dst_ref=land.at[slot, rows],
+            send_sem=send_sem.at[part, slot],
+            recv_sem=recv_sem.at[part, slot],
             device_id=(to_blk, to_rep),
             device_id_type=MESH,
         )
 
     sent = []
-    for index, combo in enumerate(combos(steps[1:])):
-        out = copy(0, combo, index)
-        out.start()
-        sent.append(out)
-    for at in range(len(steps)):
-        later = combos(steps[at + 2:])
-        for index, combo in enumerate(combos(steps[at + 1:])):
-            copy(at, combo, index).wait_recv()
-            at_rep, at_blk = place(rep, blk, combo)
-            held = part_ref if at == 0 else acc
-            total = held[at_rep, at_blk] + land[base[at] + index]
-            if at == len(steps) - 1:
-                out_ref[...] = total
-            else:
-                acc[at_rep, at_blk] = total
-                if combo[0][1]:
-                    out = copy(at + 1, combo[1:], later.index(combo[1:]))
-                    out.start()
-                    sent.append(out)
+    for index in range(1 << (count - 1)):
+        for part, steps in enumerate(orders):
+            out = copy(part, 0, combos(steps[1:])[index], index)
+            out.start()
+            sent.append(out)
+    for at in range(count):
+        for index in range(1 << (count - 1 - at)):
+            for part, steps in enumerate(orders):
+                combo = combos(steps[at + 1:])[index]
+                copy(part, at, combo, index).wait_recv()
+                at_rep, at_blk = place(rep, blk, combo)
+                held = part_ref if at == 0 else acc
+                rows = pl.ds(part * share, share)
+                total = held[at_rep, at_blk, rows] + land[base[at] + index, rows]
+                if at == count - 1:
+                    out_ref[rows] = total
+                else:
+                    acc[at_rep, at_blk, rows] = total
+                    if combo[0][1]:
+                        later = combos(steps[at + 2:])
+                        out = copy(part, at + 1, combo[1:], later.index(combo[1:]))
+                        out.start()
+                        sent.append(out)
     for out in sent:
         out.wait_send()
 
 
 def gather_all(own, rep_count, blk_count):
-    steps = [("blk", b) for b in bits_of(blk_count)[::-1]] + [("rep", b) for b in bits_of(rep_count)[::-1]]
-    most = max(1, rep_count * blk_count // 2)
+    blks = [("blk", b) for b in bits_of(blk_count)[::-1]]
+    reps = [("rep", b) for b in bits_of(rep_count)[::-1]]
+    orders = [blks + reps, blks[:-1] + reps[:-1] + blks[-1:] + reps[-1:]]
+    total = rep_count * blk_count - 1
     return pl.pallas_call(
-        functools.partial(gather_kernel, steps),
+        functools.partial(gather_kernel, orders),
         out_shape=jax.ShapeDtypeStruct((rep_count, blk_count) + own.shape, own.dtype),
         in_specs=[pl.BlockSpec(memory_space=pltpu.VMEM)],
         out_specs=pl.BlockSpec(memory_space=pltpu.VMEM),
         scratch_shapes=[
-            pltpu.SemaphoreType.DMA((len(steps), most)),
-            pltpu.SemaphoreType.DMA((len(steps), most)),
+            pltpu.SemaphoreType.DMA((len(orders), total)),
+            pltpu.SemaphoreType.DMA((len(orders), total)),
         ],
         compiler_params=pltpu.CompilerParams(
             collective_id=0, has_side_effects=True, vmem_limit_bytes=40 * 1024 * 1024
@@ -160,19 +162,21 @@
 
 def reduce_all(parts):
     rep_count, blk_count = parts.shape[:2]
-    steps = [("rep", b) for b in bits_of(rep_count)] + [("blk", b) for b in bits_of(blk_count)]
+    blks = [("blk", b) for b in bits_of(blk_count)]
+    reps = [("rep", b) for b in bits_of(rep_count)]
+    orders = [reps + blks, reps[:1] + blks[:1] + reps[1:] + blks[1:]]
     total = rep_count * blk_count - 1
     piece = parts.shape[2:]
     return pl.pallas_call(
-        functools.partial(reduce_kernel, steps),
+        functools.partial(reduce_kernel, orders),
         out_shape=jax.ShapeDtypeStruct(piece, parts.dtype),
         in_specs=[pl.BlockSpec(memory_space=pltpu.VMEM)],
         out_specs=pl.BlockSpec(memory_space=pltpu.VMEM),
         scratch_shapes=[
             pltpu.VMEM(parts.shape, parts.dtype),
             pltpu.VMEM((total,) + piece, parts.dtype),
-            pltpu.SemaphoreType.DMA((total,)),
-            pltpu.SemaphoreType.DMA((total,)),
+            pltpu.SemaphoreType.DMA((len(orders), total)),
+            pltpu.SemaphoreType.DMA((len(orders), total)),
         ],
         compiler_params=pltpu.CompilerParams(
             collective_id=1, has_side_effects=True, vmem_limit_bytes=48 * 1024 * 1024
@@ -181,7 +185,7 @@
 
 
 def contract_kernel(
-    chunk, group, per_owner, cols, trip_ref, w_ref, tab_ref, x_ref, out_ref, fi, fj, fk, y1, y2, y3
+    chunk, group, per_owner, cols, trip_ref, count_ref, tab_ref, x_ref, out_ref, fi, fj, fk, y1, y2, y3
 ):
     s = pl.program_id(0)
     step = pl.program_id(1)
@@ -255,12 +259,16 @@
 
     @pl.when(step == pl.num_programs(1) - 1)
     def _():
-        add_block(i, w_ref[s, 0], y1)
-        add_block(j, w_ref[s, 1], y2)
-        add_block(k, w_ref[s, 2], y3)
-
-
-def contract_all(triples, weights, table, tensor_blocks, per_owner, cols, rank):
+        apart = jnp.logical_and(i != j, j != k)
+        every = jnp.logical_and(i == j, j == k)
+        base = jnp.where(s < count_ref[0], jnp.where(apart, 2.0, 1.0), 0.0)
+        dropped = jnp.where(every, 0.0, base)
+        add_block(i, base, y1)
+        add_block(j, dropped, y2)
+        add_block(k, dropped, y3)
+
+
+def contract_all(triples, slot_count, table, tensor_blocks, per_owner, cols, rank):
     slots, edge = tensor_blocks.shape[:2]
     chunk = 32
     group = 8
@@ -278,7 +286,7 @@
         out_specs=pl.BlockSpec(memory_space=pltpu.VMEM),
         scratch_shapes=[wide] * 6,
         compiler_params=pltpu.CompilerParams(vmem_limit_bytes=48 * 1024 * 1024),
-    )(triples, weights, table, tensor_blocks)
+    )(triples, slot_count, table, tensor_blocks)
 
 
 def shards(tensor_blocks, triples, slot_count, factor):
@@ -291,10 +299,7 @@
     depth = rows // fold
     packed = factor.reshape(fold, depth, cols).transpose(1, 0, 2).reshape(depth, fold * cols)
     table = gather_all(packed, rep_count, blk_count)
-    slot_total = tensor_blocks.shape[0]
-    alive = (jnp.arange(slot_total, dtype=jnp.int32) < slot_count[0]).astype(jnp.float32)
-    weights = side_weights(triples) * alive[:, None]
-    parts = contract_all(triples, weights, table, tensor_blocks, rows // edge, cols, rank)
+    parts = contract_all(triples, slot_count, table, tensor_blocks, rows // edge, cols, rank)
     moment = reduce_all(parts)
     moment = moment.reshape(depth, fold, cols).transpose(1, 0, 2).reshape(rows, cols)
 

time: 66.3 us -> 59.5 us (0.90)
  Pallas kernels: 60.9 us -> 55.1 us
  other arithmetic: 1.05 us -> 0.1 us
    pallas_call x2, Pallas kernels: 43.4 us -> 37.7 us  [the longest x1 19.3 us: reduce_all(): pl.pallas_call(functools.partial(reduce_kernel, orders), out_shape=jax.Sh...]
    select_n x2 -> x0, other arithmetic: 0.88 us -> none  [the longest x1 0.87 us: side_weights(): base = jnp.where(apart, 2.0, 1.0).astype(jnp.float32)]
where the time goes in v3:
time: 59.5 us; the launch traced here: 59.3 us
  Pallas kernels  55.1 us (93%)
  local copies, waits for them, and re-layouts  2.17 us (4%)
  matrix products  1.18 us (2%)
  between operations  0.74 us (1%)
    pallas_call x1, Pallas kernels, reduce_all(): pl.pallas_call(functools.partial(reduce_kernel, orders), out_shape=jax.Sh...  19.3 us
    pallas_call x1, Pallas kernels, gather_all(): pl.pallas_call(functools.partial(gather_kernel, orders), out_shape=jax.Sh...  18.4 us
    pallas_call x1, Pallas kernels, contract_all(): pl.pallas_call(functools.partial(contract_kernel, chunk, group, per_owner...  17.4 us

profile of v3, /device:TPU:0, one launch (start us, length us, event | category | flops | bytes accessed | tf_op | source)
XLA Modules:
  0.0 59.3 jit_solution(16408654573444849122)
XLA Ops:
  0.7 0.8 %reshape.24 = bf16[2,128,64]{1,0,2:T(2,128)(2,1)S(1)} reshape(bf16[256,64]{0,1:T(8,128)(2,1)} %param.7) | data formatting | bytes 65536 | tf_op jit(solution)/shard_map/reshape | solution.py:300
  1.4 0.1 copy.16.own_ref
  1.6 18.4 %shard_map.46.tab_ref = bf16[4,8,128,128]{3,2,1,0:T(8,128)(2,1)S(1)} custom-call(bf16[128,128]{1,0:T(8,128)(2,1)S(1)} %copy.16.own_ref), custom_call_target="tpu_custom_call" | custom-call | tf_op jit(solution)/shard_map/pallas_call | solution.py:148
  20.0 0.1 copy.17
  20.1 0.1 copy.18
  20.2 0.3 convolution_bitcast_fusion
  20.6 0.1 fusion.4
  20.7 0.1 copy.20
  20.8 0.1 mul.7
  20.9 0.0 copy-start
  20.9 0.7 %copy-done = s32[2,3]{1,0:T(2,128)S(1)} copy-done((s32[2,3]{1,0:T(2,128)S(1)}, s32[2,3]{1,0:T(2,128)}, u32[]{:S(2)}) %copy-start) | copy-done | bytes 48
  21.6 17.4 %shard_map.47.part_ref = f32[4,8,128,128]{3,2,1,0:T(8,128)S(1)} custom-call(s32[2,3]{1,0:T(2,128)S(1)} %copy-done, s32[1]{0:T(128)S(6)} %copy.30.count_ref, bf16[4,8,128,128]{3,2,1,0:T(8,128)(2,1)S(1)} %shard_map.46.tab_ref, bf16[2,128,128,128]{3,2,1,0:T(8,128)(2,1)} %x_ref.1), custom_call_target="tpu_custom_call" | custom-call | tf_op jit(solution)/shard_map/pallas_call | solution.py:276
  39.1 19.3 %shard_map.48 = f32[128,128]{1,0:T(8,128)S(1)} custom-call(f32[4,8,128,128]{3,2,1,0:T(8,128)S(1)} %shard_map.47.part_ref), custom_call_target="tpu_custom_call" | custom-call | tf_op jit(solution)/shard_map/pallas_call | solution.py:170
  58.4 0.1 copy.21
  58.5 0.8 %convolution_subtract_fusion = f32[256,64]{0,1:T(8,128)} fusion(f32[256,64]{0,1:T(8,128)S(1)} %mul.7, bf16[32,8,2,128]{3,2,1,0:T(2,128)(2,1)S(1)} %bitcast.33, f32[2,8,8,128]{3,2,1,0:T(8,128)S(1)} %bitcast.35), kind=kOutput, calls=%fused_computation.1 | convolution fusion | flops 50348032 | bytes 327680 | tf_op jit(solution)/shard_map/dot_general | solution.py:316
  (2 shorter events, 0.0 us)
Async XLA Ops:
  20.9 0.7 %copy-start = (s32[2,3]{1,0:T(2,128)S(1)}, s32[2,3]{1,0:T(2,128)}, u32[]{:S(2)}) copy-start(s32[2,3]{1,0:T(2,128)} %trip_ref.1) | copy-start | bytes 76

commit v4 on v3

--- a/solution.py
+++ b/solution.py
@@ -240,21 +240,23 @@
     def _(g):
         start = pl.multiple_of(step * chunk + g * group, group)
         scale = fi[pl.ds(start, group), :]
+        third = y3[...]
+        for u in range(group):
+            right = lax.dot_general(
+                x_ref[0, g * group + u],
+                middle,
+                (((0,), (0,)), ((), ())),
+                preferred_element_type=jnp.float32,
+            )
+            third = third + right * scale[u : u + 1, :]
+        y3[...] = third
         rows = []
         second = y2[...]
-        third = y3[...]
         for u in range(group):
-            block = x_ref[0, g * group + u]
-            left = jnp.dot(block, lower, preferred_element_type=jnp.float32)
-            right = lax.dot_general(
-                block, middle, (((0,), (0,)), ((), ())), preferred_element_type=jnp.float32
-            )
-            line = scale[u : u + 1, :]
-            second = second + left * line
-            third = third + right * line
+            left = jnp.dot(x_ref[0, g * group + u], lower, preferred_element_type=jnp.float32)
+            second = second + left * scale[u : u + 1, :]
             rows.append(jnp.sum(left * fj[...], axis=0, keepdims=True))
         y2[...] = second
-        y3[...] = third
         y1[pl.ds(start, group), :] = jnp.concatenate(rows, axis=0)
 
     @pl.when(step == pl.num_programs(1) - 1)

time: 59.5 us -> 60.7 us (1.020)
  Pallas kernels: 55.1 us -> 56.3 us
    pallas_call x1, Pallas kernels: 17.4 us -> 18.6 us  [contract_all(): pl.pallas_call(functools.partial(contract_kernel, chunk, group, per_owner...]
where the time goes in v4:
time: 60.7 us; the launch traced here: 60.5 us
  Pallas kernels  56.3 us (93%)
  local copies, waits for them, and re-layouts  2.17 us (4%)
  matrix products  1.18 us (2%)
  between operations  0.74 us (1%)
    pallas_call x1, Pallas kernels, reduce_all(): pl.pallas_call(functools.partial(reduce_kernel, orders), out_shape=jax.Sh...  19.3 us
    pallas_call x1, Pallas kernels, contract_all(): pl.pallas_call(functools.partial(contract_kernel, chunk, group, per_owner...  18.6 us
    pallas_call x1, Pallas kernels, gather_all(): pl.pallas_call(functools.partial(gather_kernel, orders), out_shape=jax.Sh...  18.4 us

profile of v4, /device:TPU:0, one launch (start us, length us, event | category | flops | bytes accessed | tf_op | source)
XLA Modules:
  0.0 60.5 jit_solution(2215854298036695227)
XLA Ops:
  0.7 0.8 %reshape.24 = bf16[2,128,64]{1,0,2:T(2,128)(2,1)S(1)} reshape(bf16[256,64]{0,1:T(8,128)(2,1)} %param.7) | data formatting | bytes 65536 | tf_op jit(solution)/shard_map/reshape | solution.py:302
  1.4 0.1 copy.16.own_ref
  1.6 18.4 %shard_map.46.tab_ref = bf16[4,8,128,128]{3,2,1,0:T(8,128)(2,1)S(1)} custom-call(bf16[128,128]{1,0:T(8,128)(2,1)S(1)} %copy.16.own_ref), custom_call_target="tpu_custom_call" | custom-call | tf_op jit(solution)/shard_map/pallas_call | solution.py:148
  20.0 0.1 copy.17
  20.1 0.1 copy.18
  20.2 0.3 convolution_bitcast_fusion
  20.6 0.1 fusion.4
  20.7 0.1 copy.20
  20.8 0.1 mul.7
  20.9 0.0 copy-start
  20.9 0.7 %copy-done = s32[2,3]{1,0:T(2,128)S(1)} copy-done((s32[2,3]{1,0:T(2,128)S(1)}, s32[2,3]{1,0:T(2,128)}, u32[]{:S(2)}) %copy-start) | copy-done | bytes 48
  21.6 18.6 %shard_map.47.part_ref = f32[4,8,128,128]{3,2,1,0:T(8,128)S(1)} custom-call(s32[2,3]{1,0:T(2,128)S(1)} %copy-done, s32[1]{0:T(128)S(6)} %copy.30.count_ref, bf16[4,8,128,128]{3,2,1,0:T(8,128)(2,1)S(1)} %shard_map.46.tab_ref, bf16[2,128,128,128]{3,2,1,0:T(8,128)(2,1)} %x_ref.1), custom_call_target="tpu_custom_call" | custom-call | tf_op jit(solution)/shard_map/pallas_call | solution.py:278
  40.2 19.3 %shard_map.48 = f32[128,128]{1,0:T(8,128)S(1)} custom-call(f32[4,8,128,128]{3,2,1,0:T(8,128)S(1)} %shard_map.47.part_ref), custom_call_target="tpu_custom_call" | custom-call | tf_op jit(solution)/shard_map/pallas_call | solution.py:170
  59.5 0.1 copy.21
  59.6 0.8 %convolution_subtract_fusion = f32[256,64]{0,1:T(8,128)} fusion(f32[256,64]{0,1:T(8,128)S(1)} %mul.7, bf16[32,8,2,128]{3,2,1,0:T(2,128)(2,1)S(1)} %bitcast.33, f32[2,8,8,128]{3,2,1,0:T(8,128)S(1)} %bitcast.35), kind=kOutput, calls=%fused_computation.1 | convolution fusion | flops 50348032 | bytes 327680 | tf_op jit(solution)/shard_map/dot_general | solution.py:318
  (2 shorter events, 0.0 us)
Async XLA Ops:
  20.9 0.7 %copy-start = (s32[2,3]{1,0:T(2,128)S(1)}, s32[2,3]{1,0:T(2,128)}, u32[]{:S(2)}) copy-start(s32[2,3]{1,0:T(2,128)} %trip_ref.1) | copy-start | bytes 76
